TPU v7x, 32 devices: a whole 2x2x4 slice. The times are simulated.
32 devices in a mesh: prow: 16 (over z, y, core), pcol: 2 (over x).
Axes of the slice: x: 2, y: 2, z: 4, core: 2. Of those that a mesh axis runs over, the one named last changes fastest.
Arguments:
- inverse: float32 [2048, 2048], P('prow', 'pcol'), may hold values from -12 to 12, as said below
- factor_one: bfloat16 [2048, 512], P('prow'), may hold values from -0.1875 to 0.1875
- factor_two: bfloat16 [2048, 512], P('prow'), may hold values from -0.1875 to 0.1875
- factor_top: bfloat16 [512, 512], replicated, may hold values from -0.1875 to 0.1875
- diag_one: float32 [512, 512], replicated, may hold values from -2 to 4, as said below
- diag_two: float32 [512, 512], replicated, may hold values from -2 to 4, as said below
- pattern: int32 [2, 8], replicated, may hold values from 0 to 15, as said below
Outputs:
- inv_cols_one: float32 [2048, 512], P(('prow', 'pcol'))
- diag_block_one: float32 [512, 512], replicated
- inv_cols_two: float32 [2048, 512], P(('prow', 'pcol'))
- inv_top_two: float32 [512, 512], replicated
- diag_block_two: float32 [512, 512], replicated
Inputs may be any that keep to these rules, and one draw needn't show every extreme that they name: `pattern`: each row lists 8 distinct ancestor blocks in rising order; blocks 0 and 8 are in both rows. `inverse`: Symmetric. `diag_one`: Symmetric. `diag_two`: Symmetric.
All inputs are finite; a program needn't handle non-finite values.
Results may differ from a plain program's by a relative error of at most 0.0003.
Values may be sent and summed in bfloat16 or wider, within the bound.
A program may use at most 64 MiB of HBM per device.

v0:
```python
import jax
import jax.numpy as jnp
from jax import lax
from jax.sharding import PartitionSpec as P

BLOCK = 128


highest_precision = lax.Precision.HIGHEST


def broadcast(x, axis, root):
    mine = lax.axis_index(axis) == root
    return lax.psum(jnp.where(mine, x, jnp.zeros_like(x)), axis)


def product(left, right):
    return jnp.dot(left, right, precision=highest_precision, preferred_element_type=jnp.float32)


def row_mask(pattern_row, leading_row_index, row_count):
    row_ids = leading_row_index + lax.iota(jnp.int32, row_count)
    hits = (row_ids // BLOCK)[:, None] == pattern_row[None, :]
    return jnp.max(hits.astype(jnp.float32), axis=1)


def masked(columns, column_mask):
    return columns * column_mask[:, None].astype(jnp.bfloat16)


def multiply(inverse, columns):
    return product(inverse, columns)


def fetch_columns(factor_local, group_ratio, column_group):
    pieces = []
    for offset in range(group_ratio):
        pieces.append(broadcast(factor_local, "prow", group_ratio * column_group + offset))
    return jnp.concatenate(pieces, axis=0)


def reduce_rows(inverse, columns):
    return lax.psum_scatter(multiply(inverse, columns), "pcol", scatter_dimension=0, tiled=True)


def block_sums(inv_cols_one, own_one, own_two):
    correction = product(own_one.T, inv_cols_one)
    mirrored = product(inv_cols_one.T, own_two)
    return lax.psum((correction, mirrored), ("prow", "pcol"))


def shards(inverse, factor_one, factor_two, factor_top, diag_one, diag_two, pattern):
    row_count = inverse.shape[0]
    column_count = inverse.shape[1]
    pcol_size = lax.axis_size("pcol")
    group_ratio = lax.axis_size("prow") // pcol_size
    row_group = lax.axis_index("prow")
    column_group = lax.axis_index("pcol")
    keep_rows = row_count // pcol_size
    row_first = row_group * row_count
    column_first = column_group * column_count
    own_local = column_group * keep_rows
    own_first = row_first + own_local
    own_mask_one = row_mask(pattern[0], own_first, keep_rows)
    own_mask_two = row_mask(pattern[1], own_first, keep_rows)
    own_one = (
        lax.dynamic_slice_in_dim(factor_one, own_local, keep_rows, 0).astype(jnp.float32)
        * own_mask_one[:, None]
    )
    own_two = (
        lax.dynamic_slice_in_dim(factor_two, own_local, keep_rows, 0).astype(jnp.float32)
        * own_mask_two[:, None]
    )
    column_mask_one = row_mask(pattern[0], column_first, column_count)
    column_mask_two = row_mask(pattern[1], column_first, column_count)
    columns_one = masked(fetch_columns(factor_one, group_ratio, column_group), column_mask_one)
    share_one = reduce_rows(inverse, columns_one)
    inv_cols_one = -(own_mask_one[:, None] * share_one)
    correction_one, mirrored = block_sums(inv_cols_one, own_one, own_two)
    columns_two = masked(fetch_columns(factor_two, group_ratio, column_group), column_mask_two)
    share_two = reduce_rows(inverse, columns_two)
    diag_block_one = diag_one - correction_one
    inv_cols_two = -(own_mask_two[:, None] * (share_two + product(inv_cols_one, factor_top)))
    inv_top_two = -(mirrored + product(diag_block_one, factor_top))
    correction_two = lax.psum(product(own_two.T, inv_cols_two), ("prow", "pcol"))
    diag_block_two = diag_two - correction_two - product(factor_top.T, inv_top_two)
    return (inv_cols_one, diag_block_one, inv_cols_two, inv_top_two, diag_block_two)


def solution(mesh):
    in_specs = (P("prow", "pcol"), P("prow", None), P("prow", None), P(), P(), P(), P())
    out_specs = (P(("prow", "pcol"), None), P(), P(("prow", "pcol"), None), P(), P())
    return jax.shard_map(shards, mesh=mesh, in_specs=in_specs, out_specs=out_specs, check_vma=False)
```

profile of v0, /device:TPU:9, one launch (start us, length us, event | category | flops | bytes accessed | tf_op | source)
XLA Modules:
  0.0 306.5 jit_solution(8373516454459245324)
XLA Ops:
  7.2 0.0 copy-start
  7.2 0.0 all-reduce.7.cloned.1.call-start
  7.2 2.3 broadcast_select_fusion
  9.6 0.0 all-reduce.7.cloned.1.call-update
  9.6 0.0 reduce-scatter.7.cloned.1.call-start
  9.7 0.8 copy-done.10
  10.5 0.1 copy.31
  10.6 0.0 copy-start.26
  10.7 0.7 copy-done.26
  11.3 0.1 convert_reduce_fusion.2
  11.4 0.1 convert_reduce_fusion
  11.5 104.2 %all-reduce.7.cloned.1.call-done = (bf16[128,512]{1,0:T(8,128)(2,1)}, bf16[128,512]{1,0:T(8,128)(2,1)}, bf16[128,512]{1,0:T(8,128)(2,1)}, bf16[128,512]{1,0:T(8,...) async-done(((bf16[128,512]{1,0:T(8,128)(2,1)}, ...) | async-done | bytes 2097168 | tf_op jit(solution)/shard_map/psum | solution.py:14
  115.7 0.9 constant_dynamic-update-slice_fusion.7
  116.6 0.0 copy-done.25
  116.7 0.9 copy-done.24
  117.6 0.9 copy-done.23
  118.5 0.0 copy-done.22
  118.5 0.8 copy-done.21
  119.4 0.0 copy-done.20
  119.4 0.9 copy-done.19
  120.3 0.0 copy-done.3
  120.3 1.4 convolution_bitcast_fusion.2
  121.8 0.8 copy.27
  122.6 0.0 reduce-scatter.7.cloned.1.call-update
  122.6 0.0 reduce-scatter.9.cloned.1.call-start
  122.7 0.8 copy-done.18
  123.5 0.9 copy-done.17
  124.4 0.9 copy-done.16
  125.3 0.9 copy-done.15
  126.2 0.9 copy-done.14
  127.1 0.9 copy-done.13
  128.0 0.9 copy-done.12
  128.9 0.9 copy-done.11
  129.8 1.4 convolution_bitcast_fusion.1
  131.2 0.8 copy.29
  132.1 0.0 reduce-scatter.9.cloned.1.call-update
  132.1 0.0 all-reduce.5.cloned.1.call-start
  132.2 3.5 %reduce-scatter.7.cloned.1.call-done = f32[64,512]{1,0:T(8,128)} async-done(((f32[128,512]{1,0:T(8,128)}), f32[64,512]{1,0:T(8,128)}) %reduce-scatter.7.cloned.1.call-update) | async-done | bytes 131088
  135.7 1.0 copy.28
  136.7 0.0 copy-start.8
  136.8 0.9 copy-done.8
  137.6 2.0 fusion.12
  139.7 2.0 fusion.8
  141.6 8.6 %reduce-scatter.9.cloned.1.call-done = f32[64,512]{1,0:T(8,128)} async-done(((f32[128,512]{1,0:T(8,128)}), f32[64,512]{1,0:T(8,128)}) %reduce-scatter.9.cloned.1.call-update) | async-done | bytes 131088 | tf_op jit(solution)/shard_map/reduce_scatter | solution.py:43
  150.2 0.0 copy-done
  150.2 1.3 fusion.3
  151.5 0.0 copy-start.9
  151.5 2.1 fusion.11
  153.6 0.0 copy-done.9
  153.6 0.0 all-reduce.5.cloned.1.call-update
  153.6 0.8 copy.25
  154.4 139.9 %all-reduce.5.cloned.1.call-done = (f32[512,512]{1,0:T(8,128)}, f32[512,512]{1,0:T(8,128)}, f32[512,512]{1,0:T(8,128)}) async-done(((f32[512,512]{1,0:T(8,128)}, f32[512,512]{1,0:T(8,128)}, f32[512,512]{1,0:T(8,128)}), (f32[512,512]{1,0:T(8,128)}, f32[512,512]{1,0:T(8,128)}, f32[512,512]{1,0:T(8,128)})) %all-reduce.5.cloned.1.call-update) | async-done | bytes 3145744 | tf_op jit(solution)/shard_map/psum | solution.py:49
  294.3 0.0 copy-done.4
  294.3 1.5 sub.27
  295.9 0.0 copy-start.1
  295.9 0.0 copy-done.5
  295.9 0.0 copy-start.6
  295.9 0.0 copy-start.7
  295.9 1.0 fusion
  296.9 0.0 copy-done.1
  296.9 0.0 copy-start.2
  296.9 0.6 copy-done.6
  297.5 0.3 copy-done.7
  297.8 2.1 fusion.1
  (40 shorter events, 0.2 us)
Async XLA Ops:
  7.2 143.1 %copy-start = (bf16[512,512]{1,0:T(8,128)(2,1)S(1)}, bf16[512,512]{1,0:T(8,128)(2,1)}, u32[]{:S(2)}) copy-start(bf16[512,512]{1,0:T(8,128)(2,1)} %param.10) | copy-start | bytes 1572868
  7.2 108.5 %all-reduce.7.cloned.1.call-start = ((), (), s32[]{:S(2)}) async-start(), calls=%async_computation.5 | async-start | bytes 4194304 | tf_op jit(solution)/shard_map/psum | solution.py:14
  9.6 0.9 copy-start.10
  9.6 126.1 %reduce-scatter.7.cloned.1.call-start = ((), (), s32[]{:S(2)}) async-start(), calls=%async_computation.2 | async-start | bytes 393216
  10.6 0.7 copy-start.26
  115.7 1.0 copy-start.25
  116.6 0.9 copy-start.24
  117.5 0.9 copy-start.23
  117.5 1.0 copy-start.22
  118.4 0.9 copy-start.21
  118.4 1.0 copy-start.20
  118.5 1.8 copy-start.3
  119.4 0.9 copy-start.19
  122.6 0.9 copy-start.18
  122.6 27.6 %reduce-scatter.9.cloned.1.call-start = ((), (), s32[]{:S(2)}) async-start(), calls=%async_computation.3 | async-start | bytes 393216 | tf_op jit(solution)/shard_map/reduce_scatter | solution.py:43
  123.5 0.9 copy-start.17
  124.4 0.9 copy-start.16
  125.3 0.9 copy-start.15
  126.2 0.9 copy-start.14
  127.1 0.9 copy-start.13
  128.0 0.9 copy-start.12
  128.9 0.9 copy-start.11
  132.1 162.2 %all-reduce.5.cloned.1.call-start = ((), (), s32[]{:S(2)}) async-start(), calls=%async_computation.4 | async-start | bytes 6291456 | tf_op jit(solution)/shard_map/psum | solution.py:49
  136.7 0.9 copy-start.8
  151.5 2.1 copy-start.9
  153.6 140.7 %copy-start.4 = (f32[512,512]{1,0:T(8,128)S(1)}, f32[512,512]{1,0:T(8,128)}, u32[]{:S(2)}) copy-start(f32[512,512]{1,0:T(8,128)} %param.11) | copy-start | bytes 3145732
  294.3 1.5 copy-start.5
  295.9 1.0 copy-start.1
  295.9 1.6 copy-start.6
  295.9 1.9 copy-start.7
  296.9 3.0 copy-start.2
Sparse Core Ops, SparseCore 0:
  14.0 101.6 all-reduce.6
  122.7 12.9 reduce-scatter.6
  138.5 11.6 reduce-scatter.8
  157.4 136.8 all-reduce.4
where the time goes:
time: 310 us; the launch traced here: 306 us
  waiting for transfers between devices  256 us (83%)
  local copies, waits for them, and re-layouts  18.6 us (6%)
  between operations  14 us (5%)
  matrix products  13.3 us (4%)
  other arithmetic  4.09 us (1%)
    psum x1, waiting for transfers between devices, block_sums(): return lax.psum((correction, mirrored), ('prow', 'pcol'))  140 us
    psum x1, waiting for transfers between devices, broadcast(): return lax.psum(jnp.where(mine, x, jnp.zeros_like(x)), axis)  104 us
    unnamed x73, local copies, waits for them, and re-layouts  18.6 us
    dot_general x8, matrix products, product(): jnp.dot(left, right, precision=highest_precision, preferred_element_type=...  13.3 us
    reduce_scatter x1, waiting for transfers between devices, reduce_rows(): lax.psum_scatter(multiply(inverse, columns), 'pcol', scatter_dimension=0,...  8.6 us
  transfers between devices with their start and end apart: 4, of which 4 were waited for; matrix products, arithmetic and copies ran while one was open for 3% of the time, Pallas kernels for 0%

commit v1 on v0

v1 whole, which is shorter than its diff:
```python
import jax
import jax.numpy as jnp
from jax import lax
from jax.experimental import pallas as pl
from jax.experimental.pallas import tpu as pltpu
from jax.sharding import PartitionSpec as P

BLOCK = 128


def row_mask(pattern_row, leading_row_index, row_count):
    row_ids = leading_row_index + lax.iota(jnp.int32, row_count)
    hits = (row_ids // BLOCK)[:, None] == pattern_row[None, :]
    return jnp.max(hits.astype(jnp.float32), axis=1)


def split(x):
    high = lax.reduce_precision(x, 8, 7).astype(jnp.bfloat16)
    low = (x - high.astype(jnp.float32)).astype(jnp.bfloat16)
    return high, low


def dot(left, right, dims):
    return lax.dot_general(left, right, (dims, ((), ())), preferred_element_type=jnp.float32)


def dot_left(left, right, dims=((1,), (0,))):
    high, low = split(left)
    return dot(high, right, dims) + dot(low, right, dims)


def dot_right(left, right, dims=((1,), (0,))):
    high, low = split(right)
    return dot(left, high, dims) + dot(left, low, dims)


def finish(shares, own_mask_one, own_mask_two, sums, factor_top, diag_one, diag_two):
    width = factor_top.shape[0]
    inv_cols_one = -(own_mask_one[:, None] * shares[:, :width])
    inv_cols_two = -(own_mask_two[:, None] * (shares[:, width:] + dot_left(inv_cols_one, factor_top)))
    diag_block_one = diag_one + sums[:, :width]
    mirrored = sums[:, width : 2 * width]
    inv_top_two = mirrored - dot_left(diag_block_one, factor_top)
    diag_block_two = (
        diag_two
        + sums[:, 2 * width :]
        - dot_left(mirrored, factor_top, ((0,), (0,)))
        - dot_right(factor_top, inv_top_two, ((0,), (0,)))
    )
    return inv_cols_one, diag_block_one, inv_cols_two, inv_top_two, diag_block_two


def shards(inverse, factor_one, factor_two, factor_top, diag_one, diag_two, pattern):
    row_count, column_count = inverse.shape
    width = factor_top.shape[0]
    pcol_size = lax.axis_size("pcol")
    row_group = lax.axis_index("prow")
    column_group = lax.axis_index("pcol")
    keep_rows = row_count // pcol_size
    row_first = row_group * row_count
    own_local = column_group * keep_rows
    mask_one = row_mask(pattern[0], row_first, row_count)
    mask_two = row_mask(pattern[1], row_first, row_count)
    lead = jnp.concatenate(
        [
            factor_one * mask_one[:, None].astype(jnp.bfloat16),
            factor_two * mask_two[:, None].astype(jnp.bfloat16),
        ],
        axis=1,
    )
    own = lambda x: lax.dynamic_slice_in_dim(x, own_local, keep_rows, 0)
    leads = lax.all_gather(lead, "prow", axis=0, tiled=True)
    leads = lax.dynamic_slice_in_dim(leads, column_group * column_count, column_count, 0)
    shares = lax.psum_scatter(dot_left(inverse, leads), "pcol", scatter_dimension=0, tiled=True)
    own_lead, own_one, own_two = own(lead), own(mask_one), own(mask_two)
    first = dot_left(own_one[:, None] * shares[:, :width], own_lead, ((0,), (0,)))
    second = dot_left(shares[:, width:], own_lead[:, width:], ((0,), (0,)))
    sums = lax.psum(jnp.concatenate([first, second], axis=1), ("prow", "pcol"))
    return finish(shares, own_one, own_two, sums, factor_top, diag_one, diag_two)


MESH = pl.DeviceIdType.MESH
VMEM = pl.BlockSpec(memory_space=pltpu.VMEM)


def split_here(x):
    high = x.astype(jnp.bfloat16)
    return high, (x - high.astype(jnp.float32)).astype(jnp.bfloat16)


def exchange(
    inv_ref, lead_ref, mask_ref, y_ref, g_ref,
    leads, part_out, part_in, turned, slabs, sums_out, sums_in,
    fs_z, fs_b, fs_y, fs_c, fr_z, fr_y, fr_c,
    ps, pr, ts, tr, ss, sr, gs_z, gs_y, gs_x, gs_c, gr,
):
    p = lax.axis_index("prow")
    c = lax.axis_index("pcol")
    z, y, core = p // 4, (p // 2) % 2, p % 2
    rows = lead_ref.shape[1]
    half = rows // 2

    def at(z_, y_, core_):
        return (z_ * 2 + y_) * 2 + core_

    def remote(src, dst, send, recv, prow, pcol):
        return pltpu.make_async_remote_copy(
            src_ref=src, dst_ref=dst, send_sem=send, recv_sem=recv,
            device_id=(prow, pcol), device_id_type=MESH,
        )

    barrier = pltpu.get_barrier_semaphore()

    def greet(i, carry):
        other = lax.rem(p * 2 + c + i, 32)
        pl.semaphore_signal(barrier, inc=1, device_id=(other // 2, other % 2), device_id_type=MESH)
        return carry

    lax.fori_loop(1, 32, greet, 0)
    pl.semaphore_wait(barrier, 31)

    w = (1 - c) * z + c * (3 - z)
    step = 1 - 2 * c
    y_peer, c_peer = at(z, 1 - y, core), at(z, y, 1 - core)

    def block(s, y_, core_):
        low = (1 - c) * s + c * (1 - s)
        return at(low, y_, core_)

    def place(f, b):
        return leads.at[f, pl.ds(pl.multiple_of(b * rows, rows), rows), :]

    def fz(s, f, src):
        dst = place(f, block(s, y, core))
        return remote(src, dst, fs_z.at[s, f], fr_z.at[s, f], p + 4 * step, c)

    def fback(f):
        dst = place(f, block(1, y, core))
        return remote(lead_ref.at[f], dst, fs_b.at[f], fr_z.at[1, f], p - 4 * step, c)

    def fy(s, f, src):
        return remote(src, place(f, block(s, y, core)), fs_y.at[s, f], fr_y.at[s, f], y_peer, c)

    def fc(s, k, f, src):
        y_ = lax.rem(y + k, 2)
        return remote(src, place(f, block(s, y_, core)), fs_c.at[s, k, f], fr_c.at[s, k, f], c_peer, c)

    for s in (1, 0):
        @pl.when(w == s)
        def _(s=s):
            for f in (0, 1):
                fz(s, f, lead_ref.at[f]).start()
                fy(s, f, lead_ref.at[f]).start()
                if s == 1:
                    fback(f).start()
                fc(s, 0, f, lead_ref.at[f]).start()
            for f in (0, 1):
                leads[f, pl.ds(pl.multiple_of(block(s, y, core) * rows, rows), rows), :] = lead_ref[f]

    for s in (1, 0):
        for f in (0, 1):
            @pl.when(w != s)
            def _(s=s, f=f):
                mine = place(f, block(s, y, core))
                fz(s, f, mine).wait_recv()

                @pl.when((w == 2) | (w == s + 1))
                def _():
                    fz(s, f, mine).start()

                fy(s, f, mine).start()
                fc(s, 0, f, mine).start()

    for s in (1, 0):
        for f in (0, 1):
            theirs = place(f, block(s, 1 - y, core))
            fy(s, f, theirs).wait_recv()
            fc(s, 1, f, theirs).start()

    for s in (1, 0):
        for k in (0, 1):
            for f in (0, 1):
                fc(s, k, f, place(f, block(s, 0, core))).wait_recv()

    both = jnp.concatenate(split_here(inv_ref[...]), axis=0)
    for f in (0, 1):
        wide = dot(both, leads[f], ((1,), (0,)))
        part = wide[:rows] + wide[rows:]
        part_out[f, 0] = part[:half]
        part_out[f, 1] = part[half:]
        remote(part_out.at[f, 1 - c], part_in.at[f], ps.at[f], pr.at[f], p, 1 - c).start()
    for f in (0, 1):
        remote(part_out.at[f, 1 - c], part_in.at[f], ps.at[f], pr.at[f], p, 1 - c).wait_recv()
        y_ref[f] = part_out[f, c] + part_in[f]

    stacked = jnp.concatenate([y_ref[0] * mask_ref[:, :1], y_ref[1]], axis=0)
    turned[...] = stacked.T.reshape(16, 32, rows)
    g = p // 8
    slot = (p % 8) * 2 + c

    def column(j):
        return remote(turned.at[j], slabs.at[slot], ts.at[j], tr.at[slot], j, g)

    def send_column(i, carry):
        j = lax.rem(p + i, 16)

        @pl.when((j != p) | (g != c))
        def _():
            column(j).start()

        return carry

    lax.fori_loop(0, 16, send_column, 0)

    @pl.when(g == c)
    def _():
        slabs[slot] = turned[p]

    def take_column(q, carry):
        @pl.when((q != slot) | (g != c))
        def _():
            remote(turned.at[0], slabs.at[q], ts.at[0], tr.at[q], p, 1 - c).wait_recv()

        return carry

    lax.fori_loop(0, 16, take_column, 0)
    slab = [slabs[q] for q in range(16)]
    first = jnp.concatenate([s[:, :half] for s in slab], axis=1)
    second = jnp.concatenate([s[:, half:] for s in slab], axis=1)
    pieces = jnp.concatenate(split_here(first) + split_here(second), axis=0)
    left = dot(pieces[:64], leads[0], ((1,), (0,)))
    right = dot(pieces, leads[1], ((1,), (0,)))
    sums = jnp.concatenate(
        [left[:32] + left[32:], right[:32] + right[32:64], right[64:96] + right[96:]], axis=1
    )
    cut = sums.shape[1] // 2
    for k in (0, 1):
        for h in (0, 1):
            sums_out[k, h] = sums[16 * k : 16 * k + 16, h * cut : (h + 1) * cut]
    pair = remote(sums_out.at[1 - c], sums_in, ss, sr, p, 1 - c)
    pair.start()
    pair.wait_recv()
    me = 2 * p + c
    for h in (0, 1):
        g_ref[h, me] = sums_out[c, h] + sums_in[h]

    def chunk(z_, y_, core_, c_):
        return 2 * at(z_, y_, core_) + c_

    def gz(h, d):
        z_ = lax.rem(z + d, 4)
        return remote(g_ref.at[h, me], g_ref.at[h, me], gs_z.at[h, d - 1], gr.at[h, me], at(z_, y, core), c)

    def gy(h, o, i):
        return remote(g_ref.at[h, i], g_ref.at[h, i], gs_y.at[h, o], gr.at[h, i], y_peer, c)

    def gx(h, o, i):
        return remote(g_ref.at[h, i], g_ref.at[h, i], gs_x.at[h, o], gr.at[h, i], p, 1 - c)

    def gc(h, o, i):
        return remote(g_ref.at[h, i], g_ref.at[h, i], gs_c.at[h, o], gr.at[h, i], c_peer, c)

    for d in (1, 2, 3):
        for h in (0, 1):
            gz(h, d).start()

    def spread(d, carry):
        i = chunk(lax.rem(z + d, 4), y, core, c)
        for h in (0, 1):
            @pl.when(d > 0)
            def _(h=h):
                gy(h, 0, i).wait_recv()

            gy(h, d, i).start()
            gx(h, d, i).start()
            gc(h, d, i).start()
        return carry

    lax.fori_loop(0, 4, spread, 0)

    def relay(d, carry):
        z_ = lax.rem(z + d, 4)
        i = chunk(z_, 1 - y, core, c)
        gy(0, 0, i).wait_recv()
        gx(0, 4 + d, i).start()
        gc(0, 4 + d, i).start()
        k = chunk(z_, y, core, 1 - c)
        gx(1, 0, k).wait_recv()
        gy(1, 4 + d, k).start()
        gc(1, 4 + d, k).start()
        return carry

    lax.fori_loop(0, 4, relay, 0)

    def last(d, carry):
        z_ = lax.rem(z + d, 4)
        i = chunk(z_, y, core, 1 - c)
        gx(0, 0, i).wait_recv()
        gc(0, 8 + d, i).start()
        k = chunk(z_, 1 - y, core, c)
        gy(1, 0, k).wait_recv()
        gc(1, 8 + d, k).start()
        n = chunk(z_, 1 - y, core, 1 - c)
        gx(0, 0, n).wait_recv()
        gc(0, 12 + d, n).start()
        gy(1, 0, n).wait_recv()
        gc(1, 12 + d, n).start()
        return carry

    lax.fori_loop(0, 4, last, 0)

    def arrive(i, carry):
        n = 4 * (i // 2) + 2 * (1 - core) + i % 2
        for h in (0, 1):
            gc(h, 0, n).wait_recv()
        return carry

    lax.fori_loop(0, 16, arrive, 0)

    for s in (0, 1):
        for f in (0, 1):
            src = lead_ref.at[f]

            @pl.when((w == s) | (w == 2) | (w == s + 1))
            def _(s=s, f=f, src=src):
                fz(s, f, src).wait_send()

            fy(s, f, src).wait_send()
            for k in (0, 1):
                fc(s, k, f, src).wait_send()
    for f in (0, 1):
        @pl.when(w == 1)
        def _(f=f):
            fback(f).wait_send()

        remote(part_out.at[f, 1 - c], part_in.at[f], ps.at[f], pr.at[f], p, 1 - c).wait_send()

    def left_column(j, carry):
        @pl.when((j != p) | (g != c))
        def _():
            column(j).wait_send()

        return carry

    lax.fori_loop(0, 16, left_column, 0)
    pair.wait_send()
    for h in (0, 1):
        for d in (1, 2, 3):
            gz(h, d).wait_send()

    def left_sums(o, carry):
        for h in (0, 1):
            @pl.when(o < 8)
            def _(h=h):
                @pl.when((o < 4) | (h == 1))
                def _():
                    gy(h, o, me).wait_send()

                @pl.when((o < 4) | (h == 0))
                def _():
                    gx(h, o, me).wait_send()

            gc(h, o, me).wait_send()
        return carry

    lax.fori_loop(0, 16, left_sums, 0)


def tail_kernel(y_ref, g_ref, masks_ref, top_ref, one_ref, two_ref, c1_ref, d1_ref, c2_ref, t2_ref, d2_ref):
    width = top_ref.shape[0]
    top = top_ref[...]

    def by(left, dims=((1,), (0,))):
        high, low = split_here(left)
        return dot(high, top, dims) + dot(low, top, dims)

    c1 = -(masks_ref[0, :, :1] * y_ref[0])
    c1_ref[...] = c1
    c2_ref[...] = -(masks_ref[1, :, :1] * (y_ref[1] + by(c1)))
    cut = g_ref.shape[3]
    low = g_ref[0].reshape(width, cut)
    high = g_ref[1].reshape(width, cut)
    d1 = one_ref[...] + low[:, :width]
    d1_ref[...] = d1
    mirrored = jnp.concatenate([low[:, width:], high[:, : cut - width]], axis=1)
    t2 = mirrored - by(d1)
    t2_ref[...] = t2
    t2_high, t2_low = split_here(t2)
    top_t = top.T
    corner = dot(top_t, t2_high, ((1,), (0,))) + dot(top_t, t2_low, ((1,), (0,)))
    d2_ref[...] = two_ref[...] + high[:, cut - width :] - by(mirrored.T) - corner


def small_shards(inverse, factor_one, factor_two, factor_top, diag_one, diag_two, pattern):
    rows, columns = inverse.shape
    width = factor_top.shape[0]
    half = rows // 2
    p, c = lax.axis_index("prow"), lax.axis_index("pcol")
    masks = jnp.stack([row_mask(pattern[k], p * rows, rows) for k in (0, 1)])
    lead = jnp.stack([factor_one, factor_two]) * masks[:, :, None].astype(jnp.bfloat16)
    own = lax.dynamic_slice_in_dim(masks, c * half, half, 1)
    own = jnp.broadcast_to(own[:, :, None], (2, half, 128))
    f32, dma = jnp.float32, pltpu.SemaphoreType.DMA
    cut = 3 * width // 2
    y, g = pl.pallas_call(
        exchange,
        out_shape=(
            jax.ShapeDtypeStruct((2, half, width), f32),
            jax.ShapeDtypeStruct((2, 32, 16, cut), f32),
        ),
        in_specs=[VMEM] * 3,
        out_specs=(VMEM, VMEM),
        scratch_shapes=[
            pltpu.VMEM((2, columns, width), jnp.bfloat16),
            pltpu.VMEM((2, 2, half, width), f32),
            pltpu.VMEM((2, half, width), f32),
            pltpu.VMEM((16, 32, rows), f32),
            pltpu.VMEM((16, 32, rows), f32),
            pltpu.VMEM((2, 2, 16, cut), f32),
            pltpu.VMEM((2, 16, cut), f32),
            dma((2, 2)), dma((2,)), dma((2, 2)), dma((2, 2, 2)),
            dma((2, 2)), dma((2, 2)), dma((2, 2, 2)),
            dma((2,)), dma((2,)), dma((16,)), dma((16,)), dma, dma,
            dma((2, 3)), dma((2, 8)), dma((2, 8)), dma((2, 16)), dma((2, 32)),
        ],
        compiler_params=pltpu.CompilerParams(
            collective_id=0, has_side_effects=True, vmem_limit_bytes=48 * 2**20
        ),
    )(inverse, lead, own[0])
    square = jax.ShapeDtypeStruct((width, width), f32)
    thin = jax.ShapeDtypeStruct((half, width), f32)
    return pl.pallas_call(
        tail_kernel,
        out_shape=(thin, square, thin, square, square),
        in_specs=[VMEM] * 6,
        out_specs=(VMEM,) * 5,
        compiler_params=pltpu.CompilerParams(vmem_limit_bytes=48 * 2**20),
    )(y, g, own, factor_top, diag_one, diag_two)


def solution(mesh):
    in_specs = (P("prow", "pcol"), P("prow", None), P("prow", None), P(), P(), P(), P())
    out_specs = (P(("prow", "pcol"), None), P(), P(("prow", "pcol"), None), P(), P())
    small = mesh.shape["prow"] == 16 and mesh.shape["pcol"] == 2
    return jax.shard_map(small_shards if small else shards, mesh=mesh, in_specs=in_specs, out_specs=out_specs, check_vma=False)
```

time: 310 us -> 81.7 us (0.26); the launches traced: 306 us -> 81.4 us
  waiting for transfers between devices: 256 us -> 0 us
  Pallas kernels: 0 us -> 74 us
  between operations: 14 us -> 0.69 us
  matrix products: 13.3 us -> 0 us
  local copies, waits for them, and re-layouts: 18.6 us -> 5.51 us
    psum x2 -> x0, waiting for transfers between devices: 244 us -> none  [the longest x1 140 us: block_sums(): return lax.psum((correction, mirrored), ('prow', 'pcol'))]
    pallas_call x0 -> x2, Pallas kernels: none -> 74 us  [the longest x1 70.9 us: small_shards(): pl.pallas_call(exchange, out_shape=(jax.ShapeDtypeStruct((2, half, width)...]
    unnamed x73 -> x8, local copies, waits for them, and re-layouts: 18.6 us -> 4.52 us
    dot_general x8 -> x0, matrix products: 13.3 us -> none  [product(): jnp.dot(left, right, precision=highest_precision, preferred_element_type=...]
    reduce_scatter x1 -> x0, waiting for transfers between devices: 8.6 us -> none  [reduce_rows(): lax.psum_scatter(multiply(inverse, columns), 'pcol', scatter_dimension=0,...]
    unnamed x5 -> x0, waiting for transfers between devices: 3.61 us -> none
  transfers between devices with their start and end apart: 4 -> 0, of which waited for: 4 -> 0; matrix products, arithmetic and copies ran while one was open for 3% -> 0% of each run, Pallas kernels for 0% -> 0%
where the time goes in v1:
time: 81.7 us; the launch traced here: 81.4 us
  Pallas kernels  74 us (91%)
  local copies, waits for them, and re-layouts  5.51 us (7%)
  other arithmetic  1.2 us (1%)
    pallas_call x1, Pallas kernels, small_shards(): pl.pallas_call(exchange, out_shape=(jax.ShapeDtypeStruct((2, half, width)...  70.9 us
    unnamed x8, local copies, waits for them, and re-layouts  4.52 us
    pallas_call x1, Pallas kernels, small_shards(): pl.pallas_call(tail_kernel, out_shape=(thin, square, thin, square, square...  3.1 us

profile of v1, /device:TPU:9, one launch (start us, length us, event | category | flops | bytes accessed | tf_op | source)
XLA Modules:
  0.0 81.4 jit_solution(9360609249679561318)
XLA Ops:
  0.7 0.8 slice_bitcast_fusion.1
  1.4 0.1 convert_reduce_fusion.1
  1.5 0.1 constant_dynamic-slice_fusion
  1.6 0.1 broadcast_in_dim.14.mask_ref
  1.7 0.1 broadcast_in_dim.15.masks_ref
  1.8 1.1 %maximum_multiply_fusion.lead_ref = bf16[2,128,512]{2,1,0:T(8,128)(2,1)S(1)} fusion(bf16[1,128,512]{2,1,0:T(8,128)(2,1)} %bitcast.10, bf16[1,128,512]{2,1,0:T(8,128)(2,1)} %bitcast.11, bf16[2,128]{1,0:T(2,128)(2,1)S(1)} %fusion), kind=kLoop, calls=%fused_computation | loop fusion | flops 262144 | bytes 524800 | tf_op jit(solution)/shard_map/mul | solution.py:400
  2.8 0.0 copy-start.3
  2.9 1.0 %copy-done.3 = f32[128,1024]{1,0:T(8,128)S(1)} copy-done((f32[128,1024]{1,0:T(8,128)S(1)}, f32[128,1024]{1,0:T(8,128)}, u32[]{:S(2)}) %copy-start.3) | copy-done | bytes 524312
  3.9 70.9 %shard_map.110 = (f32[2,64,512]{2,1,0:T(8,128)S(1)}, f32[2,32,16,768]{3,2,1,0:T(8,128)S(1)}) custom-call(f32[128,1024]{1,0:T(8,128)S(1)} %copy-done.3, bf16[2,128,512]{2,1,0:T(8,128)(2,1)S(1)} %maximum_multiply_fusion.lead_ref, f32[64,128]{1,0:T(8,128)S(1)} %broadcast_in_dim.14.mask_ref), custom_call_target="tpu_custom_call" | custom-call | tf_op jit(solution)/shard_map/pallas_call | solution.py:405
  74.8 0.0 copy-start
  74.8 1.2 %copy-done = f32[512,512]{1,0:T(8,128)S(1)} copy-done((f32[512,512]{1,0:T(8,128)S(1)}, f32[512,512]{1,0:T(8,128)}, u32[]{:S(2)}) %copy-start) | copy-done | bytes 1048600
  76.0 0.0 copy-start.1
  76.0 1.2 %copy-done.1 = f32[512,512]{1,0:T(8,128)S(1)} copy-done((f32[512,512]{1,0:T(8,128)S(1)}, f32[512,512]{1,0:T(8,128)}, u32[]{:S(2)}) %copy-start.1) | copy-done | bytes 1048600
  77.2 0.0 copy-start.2
  77.2 1.0 %copy-done.2 = bf16[512,512]{1,0:T(8,128)(2,1)S(1)} copy-done((bf16[512,512]{1,0:T(8,128)(2,1)S(1)}, bf16[512,512]{1,0:T(8,128)(2,1)}, u32[]{:S(2)}) %copy-start.2) | copy-done | bytes 524312
  78.3 3.1 %shard_map.111 = (f32[64,512]{1,0:T(8,128)}, f32[512,512]{1,0:T(8,128)}, f32[64,512]{1,0:T(8,128)}, f32[512,512]{1,0:T(8,128)}, f32[512,512]{1,0:T(8,128)}) custom-call(f32[2,64,512]{2,1,0:T(8,128)S(1)} %get-tuple-element.7.y_ref, f32[2,32,16,768]{3,2,1,0:T(8,128)S(1)} %get-tuple-element.8.g_ref, f32[2,64,128]{2,1,0:T(8,128)S(1)} %broadcast_in_dim.15.masks_ref, ...), custom_call_target="tpu_custom_call" | custom-call | tf_op jit(solution)/shard_map/pallas_call | solution.py:432
  (4 shorter events, 0.0 us)
Async XLA Ops:
  2.8 1.0 %copy-start.3 = (f32[128,1024]{1,0:T(8,128)S(1)}, f32[128,1024]{1,0:T(8,128)}, u32[]{:S(2)}) copy-start(f32[128,1024]{1,0:T(8,128)} %inv_ref.1) | copy-start | bytes 1572868
  74.8 1.2 %copy-start = (f32[512,512]{1,0:T(8,128)S(1)}, f32[512,512]{1,0:T(8,128)}, u32[]{:S(2)}) copy-start(f32[512,512]{1,0:T(8,128)} %one_ref.1) | copy-start | bytes 3145732
  76.0 1.2 %copy-start.1 = (f32[512,512]{1,0:T(8,128)S(1)}, f32[512,512]{1,0:T(8,128)}, u32[]{:S(2)}) copy-start(f32[512,512]{1,0:T(8,128)} %two_ref.1) | copy-start | bytes 3145732
  77.2 1.0 %copy-start.2 = (bf16[512,512]{1,0:T(8,128)(2,1)S(1)}, bf16[512,512]{1,0:T(8,128)(2,1)}, u32[]{:S(2)}) copy-start(bf16[512,512]{1,0:T(8,128)(2,1)} %top_ref.1) | copy-start | bytes 1572868

commit v2 on v1

--- a/solution.py
+++ b/solution.py
@@ -1,3 +1,5 @@
+import functools
+
 import jax
 import jax.numpy as jnp
 from jax import lax
@@ -79,7 +81,10 @@
     return finish(shares, own_one, own_two, sums, factor_top, diag_one, diag_two)
 
 
+LEVEL = 1.0 / 16
+TOP_CODE = 32000.0
 MESH = pl.DeviceIdType.MESH
+HBM = pl.BlockSpec(memory_space=pltpu.HBM)
 VMEM = pl.BlockSpec(memory_space=pltpu.VMEM)
 
 
@@ -88,17 +93,52 @@
     return high, (x - high.astype(jnp.float32)).astype(jnp.bfloat16)
 
 
+def step_size(level):
+    return jnp.exp(level * LEVEL)
+
+
+def encode(x):
+    largest = jnp.maximum(jnp.max(jnp.abs(x), axis=1, keepdims=True), 1e-30)
+    level = jnp.ceil(jnp.log(largest) * (1.0 / LEVEL)) + 1.0
+    codes = jnp.round(x * (TOP_CODE / step_size(level)))
+    levels = jnp.broadcast_to(level, (x.shape[0], 128))
+    return jnp.concatenate([codes, levels], axis=1).astype(jnp.int32).astype(jnp.int16)
+
+
+def decode(q):
+    x = q.astype(jnp.float32)
+    cut = x.shape[1] - 128
+    return x[:, :cut] * (step_size(x[:, cut : cut + 1]) * (1.0 / TOP_CODE))
+
+
+def picked(pattern_ref, which, block):
+    hits = [jnp.where(pattern_ref[which, i] == block, 1.0, 0.0) for i in range(pattern_ref.shape[1])]
+    return functools.reduce(jnp.maximum, hits)
+
+
 def exchange(
-    inv_ref, lead_ref, mask_ref, y_ref, g_ref,
-    leads, part_out, part_in, turned, slabs, sums_out, sums_in,
+    inv_ref, one_hbm, two_hbm, pattern_hbm,
+    y_ref, g_ref, mask_ref,
+    one_ref, two_ref, pattern_ref, load_sem,
+    lead_ref, inv, inv_sem, leads, part_out, part_in, turned, slabs, sums_out, sums_in,
     fs_z, fs_b, fs_y, fs_c, fr_z, fr_y, fr_c,
-    ps, pr, ts, tr, ss, sr, gs_z, gs_y, gs_x, gs_c, gr,
+    ps, pr, ts, tr, ss, sr, gs_z, gs, gs_c, gr_z, gr, gr_c,
 ):
     p = lax.axis_index("prow")
     c = lax.axis_index("pcol")
     z, y, core = p // 4, (p // 2) % 2, p % 2
     rows = lead_ref.shape[1]
     half = rows // 2
+    loads = [
+        pltpu.make_async_copy(src, dst, load_sem.at[i])
+        for i, (src, dst) in enumerate([
+            (pattern_hbm, pattern_ref), (one_hbm, one_ref), (two_hbm, two_ref),
+        ])
+    ]
+    fetch = pltpu.make_async_copy(inv_ref, inv, inv_sem)
+    for load in loads:
+        load.start()
+    fetch.start()
 
     def at(z_, y_, core_):
         return (z_ * 2 + y_) * 2 + core_
@@ -117,6 +157,12 @@
         return carry
 
     lax.fori_loop(1, 32, greet, 0)
+    for load in loads:
+        load.wait()
+    mask_one = picked(pattern_ref, 0, p)
+    mask_ref[...] = jnp.full(mask_ref.shape, picked(pattern_ref, 1, p), jnp.float32)
+    lead_ref[0] = (one_ref[...].astype(jnp.float32) * mask_one).astype(jnp.bfloat16)
+    lead_ref[1] = (two_ref[...].astype(jnp.float32) * picked(pattern_ref, 1, p)).astype(jnp.bfloat16)
     pl.semaphore_wait(barrier, 31)
 
     w = (1 - c) * z + c * (3 - z)
@@ -157,10 +203,10 @@
             for f in (0, 1):
                 leads[f, pl.ds(pl.multiple_of(block(s, y, core) * rows, rows), rows), :] = lead_ref[f]
 
-    for s in (1, 0):
-        for f in (0, 1):
+    def along_z(f):
+        for s in (1, 0):
             @pl.when(w != s)
-            def _(s=s, f=f):
+            def _(s=s):
                 mine = place(f, block(s, y, core))
                 fz(s, f, mine).wait_recv()
 
@@ -171,29 +217,36 @@
                 fy(s, f, mine).start()
                 fc(s, 0, f, mine).start()
 
-    for s in (1, 0):
-        for f in (0, 1):
+    def from_y(f):
+        for s in (1, 0):
             theirs = place(f, block(s, 1 - y, core))
             fy(s, f, theirs).wait_recv()
             fc(s, 1, f, theirs).start()
 
-    for s in (1, 0):
-        for k in (0, 1):
-            for f in (0, 1):
+    def multiply(f):
+        for s in (1, 0):
+            for k in (0, 1):
                 fc(s, k, f, place(f, block(s, 0, core))).wait_recv()
-
-    both = jnp.concatenate(split_here(inv_ref[...]), axis=0)
-    for f in (0, 1):
         wide = dot(both, leads[f], ((1,), (0,)))
         part = wide[:rows] + wide[rows:]
         part_out[f, 0] = part[:half]
         part_out[f, 1] = part[half:]
         remote(part_out.at[f, 1 - c], part_in.at[f], ps.at[f], pr.at[f], p, 1 - c).start()
+
+    along_z(0)
+    from_y(0)
+    along_z(1)
+    fetch.wait()
+    both = jnp.concatenate(split_here(inv[...]), axis=0)
+    multiply(0)
+    from_y(1)
+    multiply(1)
     for f in (0, 1):
         remote(part_out.at[f, 1 - c], part_in.at[f], ps.at[f], pr.at[f], p, 1 - c).wait_recv()
         y_ref[f] = part_out[f, c] + part_in[f]
 
-    stacked = jnp.concatenate([y_ref[0] * mask_ref[:, :1], y_ref[1]], axis=0)
+    y_ref[0] = y_ref[0] * mask_one
+    stacked = jnp.concatenate([y_ref[0], y_ref[1]], axis=0)
     turned[...] = stacked.T.reshape(16, 32, rows)
     g = p // 8
     slot = (p % 8) * 2 + c
@@ -240,82 +293,60 @@
     pair = remote(sums_out.at[1 - c], sums_in, ss, sr, p, 1 - c)
     pair.start()
     pair.wait_recv()
-    me = 2 * p + c
-    for h in (0, 1):
-        g_ref[h, me] = sums_out[c, h] + sums_in[h]
-
-    def chunk(z_, y_, core_, c_):
-        return 2 * at(z_, y_, core_) + c_
+    def line(core_, c_, y_):
+        return ((core_ * 2 + c_) * 2 + y_) * 4
+
+    me = line(core, c, y) + z
+    for h in (0, 1):
+        g_ref[h, me] = encode(sums_out[c, h] + sums_in[h])
 
     def gz(h, d):
         z_ = lax.rem(z + d, 4)
-        return remote(g_ref.at[h, me], g_ref.at[h, me], gs_z.at[h, d - 1], gr.at[h, me], at(z_, y, core), c)
-
-    def gy(h, o, i):
-        return remote(g_ref.at[h, i], g_ref.at[h, i], gs_y.at[h, o], gr.at[h, i], y_peer, c)
-
-    def gx(h, o, i):
-        return remote(g_ref.at[h, i], g_ref.at[h, i], gs_x.at[h, o], gr.at[h, i], p, 1 - c)
-
-    def gc(h, o, i):
-        return remote(g_ref.at[h, i], g_ref.at[h, i], gs_c.at[h, o], gr.at[h, i], c_peer, c)
+        return remote(g_ref.at[h, me], g_ref.at[h, me], gs_z.at[h, d - 1], gr_z.at[h, z], at(z_, y, core), c)
+
+    def run(h, c_, y_):
+        return g_ref.at[h, pl.ds(line(core, c_, y_), 4)]
+
+    def hop(h, o, c_, y_):
+        src = run(h, c_, y_)
+        by_y = h == (o + 1) // 2 % 2
+        to = (y_peer, c) if by_y else (p, 1 - c)
+        return remote(src, src, gs.at[h, o], gr.at[h, o], to[0], to[1])
+
+    def gc(h, k):
+        src = run(h, lax.rem(c + k // 2, 2), lax.rem(y + k % 2, 2))
+        return remote(src, src, gs_c.at[h, k], gr_c.at[h, k], c_peer, c)
+
+    def relayed(h):
+        return (c, 1 - y) if h == 0 else (1 - c, y)
+
+    def second(h):
+        return (1 - c, y) if h == 0 else (c, 1 - y)
 
     for d in (1, 2, 3):
         for h in (0, 1):
             gz(h, d).start()
-
-    def spread(d, carry):
-        i = chunk(lax.rem(z + d, 4), y, core, c)
-        for h in (0, 1):
-            @pl.when(d > 0)
-            def _(h=h):
-                gy(h, 0, i).wait_recv()
-
-            gy(h, d, i).start()
-            gx(h, d, i).start()
-            gc(h, d, i).start()
-        return carry
-
-    lax.fori_loop(0, 4, spread, 0)
-
-    def relay(d, carry):
-        z_ = lax.rem(z + d, 4)
-        i = chunk(z_, 1 - y, core, c)
-        gy(0, 0, i).wait_recv()
-        gx(0, 4 + d, i).start()
-        gc(0, 4 + d, i).start()
-        k = chunk(z_, y, core, 1 - c)
-        gx(1, 0, k).wait_recv()
-        gy(1, 4 + d, k).start()
-        gc(1, 4 + d, k).start()
-        return carry
-
-    lax.fori_loop(0, 4, relay, 0)
-
-    def last(d, carry):
-        z_ = lax.rem(z + d, 4)
-        i = chunk(z_, y, core, 1 - c)
-        gx(0, 0, i).wait_recv()
-        gc(0, 8 + d, i).start()
-        k = chunk(z_, 1 - y, core, c)
-        gy(1, 0, k).wait_recv()
-        gc(1, 8 + d, k).start()
-        n = chunk(z_, 1 - y, core, 1 - c)
-        gx(0, 0, n).wait_recv()
-        gc(0, 12 + d, n).start()
-        gy(1, 0, n).wait_recv()
-        gc(1, 12 + d, n).start()
-        return carry
-
-    lax.fori_loop(0, 4, last, 0)
-
-    def arrive(i, carry):
-        n = 4 * (i // 2) + 2 * (1 - core) + i % 2
-        for h in (0, 1):
-            gc(h, 0, n).wait_recv()
-        return carry
-
-    lax.fori_loop(0, 16, arrive, 0)
+    for h in (0, 1):
+        for d in (1, 2, 3):
+            z_ = lax.rem(z + d, 4)
+            from_z = g_ref.at[h, line(core, c, y) + z_]
+            remote(from_z, from_z, gs_z.at[h, 0], gr_z.at[h, z_], c_peer, c).wait_recv()
+        hop(h, 0, c, y).start()
+        hop(h, 1, c, y).start()
+        gc(h, 0).start()
+    for h in (0, 1):
+        hop(h, 0, *relayed(h)).wait_recv()
+        hop(h, 2, *relayed(h)).start()
+        gc(h, 1 + h).start()
+    for h in (0, 1):
+        hop(h, 1, *second(h)).wait_recv()
+        gc(h, 2 - h).start()
+    for h in (0, 1):
+        hop(h, 2, 1 - c, 1 - y).wait_recv()
+        gc(h, 3).start()
+    for h in (0, 1):
+        for k in range(4):
+            gc(h, k).wait_recv()
 
     for s in (0, 1):
         for f in (0, 1):
@@ -347,26 +378,25 @@
     for h in (0, 1):
         for d in (1, 2, 3):
             gz(h, d).wait_send()
-
-    def left_sums(o, carry):
-        for h in (0, 1):
-            @pl.when(o < 8)
-            def _(h=h):
-                @pl.when((o < 4) | (h == 1))
-                def _():
-                    gy(h, o, me).wait_send()
-
-                @pl.when((o < 4) | (h == 0))
-                def _():
-                    gx(h, o, me).wait_send()
-
-            gc(h, o, me).wait_send()
-        return carry
-
-    lax.fori_loop(0, 16, left_sums, 0)
-
-
-def tail_kernel(y_ref, g_ref, masks_ref, top_ref, one_ref, two_ref, c1_ref, d1_ref, c2_ref, t2_ref, d2_ref):
+        for o in range(3):
+            hop(h, o, c, y).wait_send()
+        for k in range(4):
+            gc(h, k).wait_send()
+
+
+def tail_kernel(
+    y_hbm, mask_hbm, top_hbm, one_hbm, g_hbm, two_hbm, c1_ref, d1_ref, c2_ref, t2_ref, d2_ref,
+    y_ref, mask_ref, top_ref, one_ref, g_ref, two_ref, sem,
+):
+    pairs = [
+        (y_hbm, y_ref), (mask_hbm, mask_ref), (top_hbm, top_ref),
+        (g_hbm, g_ref), (one_hbm, one_ref), (two_hbm, two_ref),
+    ]
+    loads = [pltpu.make_async_copy(src, dst, sem.at[i]) for i, (src, dst) in enumerate(pairs)]
+    for load in loads:
+        load.start()
+    for load in loads[:3]:
+        load.wait()
     width = top_ref.shape[0]
     top = top_ref[...]
 
@@ -374,12 +404,15 @@
         high, low = split_here(left)
         return dot(high, top, dims) + dot(low, top, dims)
 
-    c1 = -(masks_ref[0, :, :1] * y_ref[0])
+    c1 = -y_ref[0]
     c1_ref[...] = c1
-    c2_ref[...] = -(masks_ref[1, :, :1] * (y_ref[1] + by(c1)))
-    cut = g_ref.shape[3]
-    low = g_ref[0].reshape(width, cut)
-    high = g_ref[1].reshape(width, cut)
+    c2_ref[...] = -(mask_ref[:1, :1] * (y_ref[1] + by(c1)))
+    for load in loads[3:]:
+        load.wait()
+    cut = g_ref.shape[3] - 128
+    order = [((core * 2 + c) * 2 + y) * 4 + z for z in range(4) for y in (0, 1) for core in (0, 1) for c in (0, 1)]
+    low = decode(jnp.concatenate([g_ref[0, i] for i in order], axis=0))
+    high = decode(jnp.concatenate([g_ref[1, i] for i in order], axis=0))
     d1 = one_ref[...] + low[:, :width]
     d1_ref[...] = d1
     mirrored = jnp.concatenate([low[:, width:], high[:, : cut - width]], axis=1)
@@ -395,22 +428,26 @@
     rows, columns = inverse.shape
     width = factor_top.shape[0]
     half = rows // 2
-    p, c = lax.axis_index("prow"), lax.axis_index("pcol")
-    masks = jnp.stack([row_mask(pattern[k], p * rows, rows) for k in (0, 1)])
-    lead = jnp.stack([factor_one, factor_two]) * masks[:, :, None].astype(jnp.bfloat16)
-    own = lax.dynamic_slice_in_dim(masks, c * half, half, 1)
-    own = jnp.broadcast_to(own[:, :, None], (2, half, 128))
     f32, dma = jnp.float32, pltpu.SemaphoreType.DMA
     cut = 3 * width // 2
-    y, g = pl.pallas_call(
+    square = jax.ShapeDtypeStruct((width, width), f32)
+    y, g, mask = pl.pallas_call(
         exchange,
         out_shape=(
             jax.ShapeDtypeStruct((2, half, width), f32),
-            jax.ShapeDtypeStruct((2, 32, 16, cut), f32),
+            jax.ShapeDtypeStruct((2, 32, 16, cut + 128), jnp.int16),
+            jax.ShapeDtypeStruct((8, 128), f32),
         ),
-        in_specs=[VMEM] * 3,
-        out_specs=(VMEM, VMEM),
+        in_specs=[HBM] * 4,
+        out_specs=(VMEM,) * 3,
         scratch_shapes=[
+            pltpu.VMEM((rows, width), jnp.bfloat16),
+            pltpu.VMEM((rows, width), jnp.bfloat16),
+            pltpu.SMEM(pattern.shape, jnp.int32),
+            dma((3,)),
+            pltpu.VMEM((2, rows, width), jnp.bfloat16),
+            pltpu.VMEM((rows, columns), f32),
+            dma,
             pltpu.VMEM((2, columns, width), jnp.bfloat16),
             pltpu.VMEM((2, 2, half, width), f32),
             pltpu.VMEM((2, half, width), f32),
@@ -421,21 +458,24 @@
             dma((2, 2)), dma((2,)), dma((2, 2)), dma((2, 2, 2)),
             dma((2, 2)), dma((2, 2)), dma((2, 2, 2)),
             dma((2,)), dma((2,)), dma((16,)), dma((16,)), dma, dma,
-            dma((2, 3)), dma((2, 8)), dma((2, 8)), dma((2, 16)), dma((2, 32)),
+            dma((2, 3)), dma((2, 3)), dma((2, 4)), dma((2, 4)), dma((2, 3)), dma((2, 4)),
         ],
         compiler_params=pltpu.CompilerParams(
-            collective_id=0, has_side_effects=True, vmem_limit_bytes=48 * 2**20
+            collective_id=0, has_side_effects=True, vmem_limit_bytes=60 * 2**20
         ),
-    )(inverse, lead, own[0])
-    square = jax.ShapeDtypeStruct((width, width), f32)
+    )(inverse, factor_one, factor_two, pattern)
     thin = jax.ShapeDtypeStruct((half, width), f32)
     return pl.pallas_call(
         tail_kernel,
         out_shape=(thin, square, thin, square, square),
-        in_specs=[VMEM] * 6,
+        in_specs=[HBM] * 6,
+        scratch_shapes=[
+            *[pltpu.VMEM(x.shape, x.dtype) for x in (y, mask, factor_top, diag_one, g, diag_two)],
+            dma((6,)),
+        ],
         out_specs=(VMEM,) * 5,
-        compiler_params=pltpu.CompilerParams(vmem_limit_bytes=48 * 2**20),
-    )(y, g, own, factor_top, diag_one, diag_two)
+        compiler_params=pltpu.CompilerParams(vmem_limit_bytes=60 * 2**20),
+    )(y, mask, factor_top, diag_one, g, diag_two)
 
 
 def solution(mesh):

time: 81.7 us -> 74.1 us (0.907); the launches traced: 81.4 us -> 72.7 us
  local copies, waits for them, and re-layouts: 5.51 us -> 0 us
  Pallas kernels: 74 us -> 72 us
  other arithmetic: 1.2 us -> 0 us
    unnamed x8 -> x0, local copies, waits for them, and re-layouts: 4.52 us -> none
    pallas_call x1, Pallas kernels: 70.9 us -> 66.7 us  [small_shards(): pl.pallas_call(exchange, out_shape=(jax.ShapeDtypeStruct((2, half, width)...]
    pallas_call x1, Pallas kernels: 3.1 us -> 5.39 us  [small_shards(): pl.pallas_call(tail_kernel, out_shape=(thin, square, thin, square, square...]
    mul x1 -> x0, other arithmetic: 1.08 us -> none  [small_shards(): jnp.stack([factor_one, factor_two]) * masks[:, :, None].astype(jnp.bfloat16)]
where the time goes in v2:
time: 74.1 us; the launch traced here: 72.7 us
  Pallas kernels  72 us (97%)
    pallas_call x1, Pallas kernels, small_shards(): pl.pallas_call(exchange, out_shape=(jax.ShapeDtypeStruct((2, half, width)...  66.7 us
    pallas_call x1, Pallas kernels, small_shards(): pl.pallas_call(tail_kernel, out_shape=(thin, square, thin, square, square...  5.39 us

profile of v2, /device:TPU:9, one launch (start us, length us, event | category | flops | bytes accessed | tf_op | source)
XLA Modules:
  0.0 72.7 jit_solution(13943832724202975226)
XLA Ops:
  0.6 66.7 %shard_map.110 = (f32[2,64,512]{2,1,0:T(8,128)}, s16[2,32,16,896]{3,2,1,0:T(8,128)(2,1)}, f32[8,128]{1,0:T(8,128)}) custom-call(f32[128,1024]{1,0:T(8,128)} %inv_ref.1, bf16[128,512]{1,0:T(8,128)(2,1)} %one_hbm.2, bf16[128,512]{1,0:T(8,128)(2,1)} %two_hbm.2, s32[2,8]{1,0:T(2,128)} %pattern_hbm.1), custom_call_target="tpu_custom_call" | custom-call | tf_op jit(solution)/shard_map/pallas_call | solution.py:434
  67.3 5.4 %shard_map.111 = (f32[64,512]{1,0:T(8,128)}, f32[512,512]{1,0:T(8,128)}, f32[64,512]{1,0:T(8,128)}, f32[512,512]{1,0:T(8,128)}, f32[512,512]{1,0:T(8,128)}) custom-call(f32[2,64,512]{2,1,0:T(8,128)} %get-tuple-element.8.y_hbm, f32[8,128]{1,0:T(8,128)} %get-tuple-element.9.mask_hbm, bf16[512,512]{1,0:T(8,128)(2,1)} %top_hbm.1, f32[512,512]{1,0:T(8,128)} %one_hbm.3, ...), custom_call_target="tpu_custom_call" | custom-call | tf_op jit(solution)/shard_map/pallas_call | solution.py:468
